TPU v7x, 512 devices: a whole 4x4x16 slice. The times are simulated.
512 devices in a mesh: freq: 16 (over y, x), patch: 32 (over z, core).
Axes of the slice: x: 4, y: 4, z: 16, core: 2. Of those that a mesh axis runs over, the one named last changes fastest.
Arguments:
- responses: bfloat16 [2048, 2, 2048], P('patch', None, 'freq'), may hold values from -6 to 6
- adjoints: bfloat16 [2048, 2, 2048], P('patch', None, 'freq'), may hold values from -6 to 6
- patch_shapes: bfloat16 [3072, 4, 48, 128], P('patch'), may hold values from -0.25 to 0.25
- block_lists: int32 [3072, 4], P('patch'), may hold values from 0 to 15
- block_counts: int32 [3072], P('patch'), may hold values from 1 to 4
- patch_sizes: int32 [3072], P('patch'), may hold values from 12 to 48
- owner_map: int32 [3072], P('patch'), may hold values from 0 to 3071, each once
Outputs:
- loss_gradient: float32 [3072], P('patch')
Inputs may be any that keep to these rules, and one draw needn't show every extreme that they name: `owner_map`: each patch appears once.
All inputs are finite; a program needn't handle non-finite values.
Results may differ from a plain program's by a relative error of at most 0.0003.
Values may be sent and summed in bfloat16 or wider, within the bound.
A program may use at most 64 MiB of HBM per device.

v0:
```python
import math
import jax
import jax.numpy as jnp
from jax import lax
from jax.sharding import PartitionSpec as P


def strain_terms(total, masked, blocks, resp_piece, adjo_piece, width):
    count = resp_piece.shape[0]
    modes = resp_piece.shape[2]
    patches = masked.shape[0]
    samples = masked.shape[2]
    step = math.gcd(count, 32)
    turns = count // step

    def one(index, carry):
        resp = lax.dynamic_slice_in_dim(resp_piece, index * step, step, 0).reshape(
            step * 2, modes // width, width
        )
        adjo = lax.dynamic_slice_in_dim(adjo_piece, index * step, step, 0).reshape(
            step * 2, modes // width, width
        )
        forward = jnp.einsum(
            "pksb,cpkb->cps", masked, resp[:, blocks, :], preferred_element_type=jnp.float32
        )
        backward = jnp.einsum(
            "pksb,cpkb->cps", masked, adjo[:, blocks, :], preferred_element_type=jnp.float32
        )
        forward = forward.reshape(step, 2, patches, samples)
        backward = backward.reshape(step, 2, patches, samples)
        cross = forward[:, 0] * backward[:, 1] - forward[:, 1] * backward[:, 0]
        return carry + jnp.sum(cross, axis=(0, 2))

    return lax.fori_loop(0, turns, one, total)


def body(responses, adjoints, patch_shapes, block_lists, block_counts, patch_sizes, owner_map):
    patch_dev, slots, samples, width = patch_shapes.shape
    slot_live = jnp.arange(slots, dtype=jnp.int32)[None, :] < block_counts[:, None]
    row_live = jnp.arange(samples, dtype=jnp.int32)[None, :] < patch_sizes[:, None]
    live = (slot_live[:, :, None, None] & row_live[:, None, :, None]).astype(jnp.bfloat16)
    masked = patch_shapes * live
    freqs = responses.shape[0] * lax.axis_size("patch")
    empty = jnp.zeros((patch_dev,), jnp.float32)
    regrouped = (
        lax.all_to_all(responses, "freq", split_axis=0, concat_axis=2, tiled=True),
        lax.all_to_all(adjoints, "freq", split_axis=0, concat_axis=2, tiled=True),
    )
    terms = strain_terms(
        empty,
        masked,
        block_lists,
        lax.all_gather(regrouped[0], "patch", axis=0, tiled=True),
        lax.all_gather(regrouped[1], "patch", axis=0, tiled=True),
        width,
    )
    terms = terms * (samples * freqs) ** (-0.5)
    patches = patch_dev * lax.axis_size("patch")
    columns = jnp.arange(patches, dtype=jnp.int32)
    onehot = (owner_map[:, None] == columns[None, :]).astype(jnp.float32)
    dense = jnp.dot(terms, onehot, precision=lax.Precision.HIGHEST)
    mine = lax.psum_scatter(dense, "patch", scatter_dimension=0, tiled=True)
    return lax.psum(mine, "freq")


def solution(mesh):
    placed = (
        P("patch", None, "freq"),
        P("patch", None, "freq"),
        P("patch", None, None, None),
        P("patch", None),
        P("patch"),
        P("patch"),
        P("patch"),
    )
    return jax.shard_map(body, mesh=mesh, in_specs=placed, out_specs=P("patch"), check_vma=False)
```

profile of v0, /device:TPU:32, one launch (start us, length us, event | category | flops | bytes accessed | tf_op | source)
XLA Modules:
  0.0 486.1 jit_solution(6683167722934066681)
XLA Ops:
  6.5 14.6 %all_to_all.36 = bf16[64,2,128]{2,1,0:T(2,128)(2,1)S(1)} all-to-all(bf16[64,2,128]{2,1,0:T(2,128)(2,1)} %param.9), channel_id=1, replica_groups=mesh['freq'=16,'patch'=32] {'freq'}, dimensions={0} | all-to-all | bytes 65536 | tf_op jit(solution)/shard_map/all_to_all | solution.py:46
  21.9 11.0 %all_to_all.37 = bf16[64,2,128]{2,1,0:T(2,128)(2,1)S(1)} all-to-all(bf16[64,2,128]{2,1,0:T(2,128)(2,1)} %param.10), channel_id=1, replica_groups=mesh['freq'=16,'patch'=32] {'freq'}, dimensions={0} | all-to-all | bytes 65536 | tf_op jit(solution)/shard_map/all_to_all | solution.py:47
  38.0 6.3 %broadcast_multiply_fusion = bf16[96,4,48,128]{3,2,1,0:T(8,128)(2,1)} fusion(bf16[96,4,48,128]{3,2,1,0:T(8,128)(2,1)} %param.11, bf16[96,4,48]{2,1,0:T(4,128)(2,1)S(1)} %and_convert_fusion), kind=kLoop, calls=%fused_computation.14 | loop fusion | flops 2359296 | bytes 9474048 | tf_op jit(solution)/shard_map/mul | solution.py:42
  44.3 48.6 %all-gather.3.cloned.1.call-done = bf16[128,2,2048]{2,1,0:T(2,128)(2,1)} async-done(((bf16[4,2,2048]{2,1,0:T(2,128)(2,1)}), bf16[128,2,2048]{2,1,0:T(2,128)(2,1)}) %all-gather.3.cloned.1.call-update) | async-done | bytes 1048592 | tf_op jit(solution)/shard_map/all_gather | solution.py:53
  92.8 70.0 %all-gather.5.cloned.1.call-done = bf16[128,2,2048]{2,1,0:T(2,128)(2,1)} async-done(((bf16[4,2,2048]{2,1,0:T(2,128)(2,1)}), bf16[128,2,2048]{2,1,0:T(2,128)(2,1)}) %all-gather.5.cloned.1.call-update) | async-done | bytes 1048592 | tf_op jit(solution)/shard_map/all_gather | solution.py:54
  162.8 185.3 %while.14 = (s32[]{:T(128)}, f32[96]{0:T(128)S(1)}, bf16[128,2,2048]{2,1,0:T(2,128)(2,1)}, s32[96,4]{1,0:T(8,128)S(1)}, bf16[96,4,48,128]{3,2,1,0:T(8,128)(2,1)}...) while((s32[]{:T(128)}, f32[96]{0:T(128)S(1)}, ...), condition=%wide.region_2.0_spmd.clone, body=%wide.region_0.0_spmd.clone.sunk | while | flops 604571840 | bytes 59785376 | solution.py:34
  164.6 13.3 %gather_fusion = bf16[384,64,128]{2,1,0:T(8,128)(2,1)} fusion(bf16[64,16,128]{2,0,1:T(8,128)(2,1)S(1)} %copy.39, s32[1024]{0:T(1024)S(1)} %pad_clamp_fusion.2), kind=kCustom, calls=%fused_computation.1.clone.clone.1 | custom fusion | bytes 12584448 | tf_op jit(solution)/shard_map/while/body/eval_jaxpr/gather | solution.py:27
  177.9 5.9 %convolution_bitcast_fusion.4 = f32[64,96,48]{0,2,1:T(8,128)S(1)} fusion(bf16[64,96,4,128]{3,0,2,1:T(8,128)(2,1)} %bitcast.66, bf16[96,4,48,128]{3,2,1,0:T(8,128)(2,1)} %get-tuple-element.233), kind=kOutput, calls=%fused_computation.2.clone.1 | convolution fusion | flops 301989888 | bytes 12189696 | tf_op jit(solution)/shard_map/while/body/eval_jaxpr/pksb,cpkb->cps/dot_general | solution.py:26
  183.9 1.9 copy.40
  186.0 13.3 %gather_fusion.1 = bf16[384,64,128]{2,1,0:T(8,128)(2,1)} fusion(bf16[64,16,128]{2,0,1:T(8,128)(2,1)S(1)} %copy.41, s32[1024]{0:T(1024)S(1)} %pad_clamp_fusion.2), kind=kCustom, calls=%fused_computation.clone.clone.1 | custom fusion | bytes 12584448 | tf_op jit(solution)/shard_map/while/body/eval_jaxpr/gather | solution.py:24
  199.3 5.9 %convolution_bitcast_fusion.5 = f32[64,96,48]{0,2,1:T(8,128)S(1)} fusion(bf16[64,96,4,128]{3,0,2,1:T(8,128)(2,1)} %bitcast.65, bf16[96,4,48,128]{3,2,1,0:T(8,128)(2,1)} %get-tuple-element.233), kind=kOutput, calls=%fused_computation.3.clone.1 | convolution fusion | flops 301989888 | bytes 12189696 | tf_op jit(solution)/shard_map/while/body/eval_jaxpr/pksb,cpkb->cps/dot_general | solution.py:23
  207.1 2.1 fusion.23
  210.9 13.3 %gather_fusion = bf16[384,64,128]{2,1,0:T(8,128)(2,1)} fusion(bf16[64,16,128]{2,0,1:T(8,128)(2,1)S(1)} %copy.39, s32[1024]{0:T(1024)S(1)} %pad_clamp_fusion.2), kind=kCustom, calls=%fused_computation.1.clone.clone.1 | custom fusion | bytes 12584448 | tf_op jit(solution)/shard_map/while/body/eval_jaxpr/gather | solution.py:27
  224.3 5.9 %convolution_bitcast_fusion.4 = f32[64,96,48]{0,2,1:T(8,128)S(1)} fusion(bf16[64,96,4,128]{3,0,2,1:T(8,128)(2,1)} %bitcast.66, bf16[96,4,48,128]{3,2,1,0:T(8,128)(2,1)} %get-tuple-element.233), kind=kOutput, calls=%fused_computation.2.clone.1 | convolution fusion | flops 301989888 | bytes 12189696 | tf_op jit(solution)/shard_map/while/body/eval_jaxpr/pksb,cpkb->cps/dot_general | solution.py:26
  230.2 1.9 copy.40
  232.3 13.3 %gather_fusion.1 = bf16[384,64,128]{2,1,0:T(8,128)(2,1)} fusion(bf16[64,16,128]{2,0,1:T(8,128)(2,1)S(1)} %copy.41, s32[1024]{0:T(1024)S(1)} %pad_clamp_fusion.2), kind=kCustom, calls=%fused_computation.clone.clone.1 | custom fusion | bytes 12584448 | tf_op jit(solution)/shard_map/while/body/eval_jaxpr/gather | solution.py:24
  245.6 5.9 %convolution_bitcast_fusion.5 = f32[64,96,48]{0,2,1:T(8,128)S(1)} fusion(bf16[64,96,4,128]{3,0,2,1:T(8,128)(2,1)} %bitcast.65, bf16[96,4,48,128]{3,2,1,0:T(8,128)(2,1)} %get-tuple-element.233), kind=kOutput, calls=%fused_computation.3.clone.1 | convolution fusion | flops 301989888 | bytes 12189696 | tf_op jit(solution)/shard_map/while/body/eval_jaxpr/pksb,cpkb->cps/dot_general | solution.py:23
  253.4 2.1 fusion.23
  257.3 13.3 %gather_fusion = bf16[384,64,128]{2,1,0:T(8,128)(2,1)} fusion(bf16[64,16,128]{2,0,1:T(8,128)(2,1)S(1)} %copy.39, s32[1024]{0:T(1024)S(1)} %pad_clamp_fusion.2), kind=kCustom, calls=%fused_computation.1.clone.clone.1 | custom fusion | bytes 12584448 | tf_op jit(solution)/shard_map/while/body/eval_jaxpr/gather | solution.py:27
  270.6 5.9 %convolution_bitcast_fusion.4 = f32[64,96,48]{0,2,1:T(8,128)S(1)} fusion(bf16[64,96,4,128]{3,0,2,1:T(8,128)(2,1)} %bitcast.66, bf16[96,4,48,128]{3,2,1,0:T(8,128)(2,1)} %get-tuple-element.233), kind=kOutput, calls=%fused_computation.2.clone.1 | convolution fusion | flops 301989888 | bytes 12189696 | tf_op jit(solution)/shard_map/while/body/eval_jaxpr/pksb,cpkb->cps/dot_general | solution.py:26
  276.5 1.9 copy.40
  278.6 13.3 %gather_fusion.1 = bf16[384,64,128]{2,1,0:T(8,128)(2,1)} fusion(bf16[64,16,128]{2,0,1:T(8,128)(2,1)S(1)} %copy.41, s32[1024]{0:T(1024)S(1)} %pad_clamp_fusion.2), kind=kCustom, calls=%fused_computation.clone.clone.1 | custom fusion | bytes 12584448 | tf_op jit(solution)/shard_map/while/body/eval_jaxpr/gather | solution.py:24
  291.9 5.9 %convolution_bitcast_fusion.5 = f32[64,96,48]{0,2,1:T(8,128)S(1)} fusion(bf16[64,96,4,128]{3,0,2,1:T(8,128)(2,1)} %bitcast.65, bf16[96,4,48,128]{3,2,1,0:T(8,128)(2,1)} %get-tuple-element.233), kind=kOutput, calls=%fused_computation.3.clone.1 | convolution fusion | flops 301989888 | bytes 12189696 | tf_op jit(solution)/shard_map/while/body/eval_jaxpr/pksb,cpkb->cps/dot_general | solution.py:23
  299.7 2.1 fusion.23
  303.6 13.3 %gather_fusion = bf16[384,64,128]{2,1,0:T(8,128)(2,1)} fusion(bf16[64,16,128]{2,0,1:T(8,128)(2,1)S(1)} %copy.39, s32[1024]{0:T(1024)S(1)} %pad_clamp_fusion.2), kind=kCustom, calls=%fused_computation.1.clone.clone.1 | custom fusion | bytes 12584448 | tf_op jit(solution)/shard_map/while/body/eval_jaxpr/gather | solution.py:27
  316.9 5.9 %convolution_bitcast_fusion.4 = f32[64,96,48]{0,2,1:T(8,128)S(1)} fusion(bf16[64,96,4,128]{3,0,2,1:T(8,128)(2,1)} %bitcast.66, bf16[96,4,48,128]{3,2,1,0:T(8,128)(2,1)} %get-tuple-element.233), kind=kOutput, calls=%fused_computation.2.clone.1 | convolution fusion | flops 301989888 | bytes 12189696 | tf_op jit(solution)/shard_map/while/body/eval_jaxpr/pksb,cpkb->cps/dot_general | solution.py:26
  322.8 1.9 copy.40
  325.0 13.3 %gather_fusion.1 = bf16[384,64,128]{2,1,0:T(8,128)(2,1)} fusion(bf16[64,16,128]{2,0,1:T(8,128)(2,1)S(1)} %copy.41, s32[1024]{0:T(1024)S(1)} %pad_clamp_fusion.2), kind=kCustom, calls=%fused_computation.clone.clone.1 | custom fusion | bytes 12584448 | tf_op jit(solution)/shard_map/while/body/eval_jaxpr/gather | solution.py:24
  338.3 5.9 %convolution_bitcast_fusion.5 = f32[64,96,48]{0,2,1:T(8,128)S(1)} fusion(bf16[64,96,4,128]{3,0,2,1:T(8,128)(2,1)} %bitcast.65, bf16[96,4,48,128]{3,2,1,0:T(8,128)(2,1)} %get-tuple-element.233), kind=kOutput, calls=%fused_computation.3.clone.1 | convolution fusion | flops 301989888 | bytes 12189696 | tf_op jit(solution)/shard_map/while/body/eval_jaxpr/pksb,cpkb->cps/dot_general | solution.py:23
  346.1 2.1 fusion.23
  348.7 89.7 %all-reduce = f32[3072]{0:T(1024)S(1)} all-reduce(f32[3072]{0:T(1024)S(1)} %bitcast.73), channel_id=2, replica_groups=mesh['freq'=16,'patch'=32] {'patch'}, use_global_device_ids=true, to_apply=%region_3.0.clone | all-reduce | flops 3072 | bytes 24576
  438.5 40.8 %psum.7 = f32[96]{0:T(128)} all-reduce(f32[96]{0:T(128)S(1)} %dynamic-slice.1), channel_id=1, replica_groups=mesh['freq'=16,'patch'=32] {'freq'}, use_global_device_ids=true, to_apply=%region_4.0 | all-reduce | flops 96 | bytes 768 | tf_op jit(solution)/shard_map/psum | solution.py:63
  (58 shorter events, 21.1 us)
Async XLA Ops:
  6.5 86.3 %all-gather.3.cloned.1.call-start = ((), (), s32[]{:S(2)}) async-start(), calls=%async_computation.2 | async-start | bytes 1081344 | tf_op jit(solution)/shard_map/all_gather | solution.py:53
  21.8 141.0 %all-gather.5.cloned.1.call-start = ((), (), s32[]{:S(2)}) async-start(), calls=%async_computation.3 | async-start | bytes 1081344 | tf_op jit(solution)/shard_map/all_gather | solution.py:54
  162.8 185.3 %copy-start = (s32[96]{0:T(128)S(1)}, s32[96]{0:T(128)}, u32[]{:S(2)}) copy-start(s32[96]{0:T(128)} %param.15) | copy-start | bytes 1156
Sparse Core Ops, SparseCore 0:
  22.0 70.8 all-gather.2
  95.0 67.8 all-gather.4
where the time goes:
time: 487 us; the launch traced here: 486 us
  blocking collectives  156 us (32%)
  local copies, waits for them, and re-layouts  133 us (27%)
  waiting for transfers between devices  119 us (24%)
  matrix products  47.9 us (10%)
  other arithmetic  16.3 us (3%)
  between operations  14.1 us (3%)
    unnamed x1, blocking collectives  89.7 us
    all_gather x1, waiting for transfers between devices, body(): lax.all_gather(regrouped[1], 'patch', axis=0, tiled=True)  70 us
    gather x4, local copies, waits for them, and re-layouts, one(): adjo[:, blocks, :]  53.2 us
    gather x4, local copies, waits for them, and re-layouts, one(): resp[:, blocks, :]  53.2 us
    all_gather x1, waiting for transfers between devices, body(): lax.all_gather(regrouped[0], 'patch', axis=0, tiled=True)  48.6 us
    psum x1, blocking collectives, body(): return lax.psum(mine, 'freq')  40.8 us
    dot_general x4, matrix products, one(): jnp.einsum('pksb,cpkb->cps', masked, adjo[:, blocks, :], preferred_elemen...  23.7 us
    dot_general x4, matrix products, one(): jnp.einsum('pksb,cpkb->cps', masked, resp[:, blocks, :], preferred_elemen...  23.7 us
  transfers between devices with their start and end apart: 2, of which 2 were waited for; matrix products, arithmetic and copies ran while one was open for 2% of the time, Pallas kernels for 0%

commit v1 on v0

--- a/solution.py
+++ b/solution.py
@@ -3,6 +3,18 @@
 import jax.numpy as jnp
 from jax import lax
 from jax.sharding import PartitionSpec as P
+
+
+def collect(x, axis, dim):
+    ways, here = (lax.axis_size(axis), lax.axis_index(axis))
+    grown, reach = (x, 1)
+    while reach < ways:
+        theirs = lax.ppermute(grown, axis, [(d, d ^ reach) for d in range(ways)])
+        mine_first = jnp.concatenate([grown, theirs], axis=dim)
+        theirs_first = jnp.concatenate([theirs, grown], axis=dim)
+        grown = jnp.where(here & reach == 0, mine_first, theirs_first)
+        reach = 2 * reach
+    return grown
 
 
 def strain_terms(total, masked, blocks, resp_piece, adjo_piece, width):
@@ -50,7 +62,7 @@
         empty,
         masked,
         block_lists,
-        lax.all_gather(regrouped[0], "patch", axis=0, tiled=True),
+        collect(regrouped[0], "patch", 0),
         lax.all_gather(regrouped[1], "patch", axis=0, tiled=True),
         width,
     )

time: 487 us -> 481 us (0.988)
  the two profiles are of different devices: /device:TPU:32 before, /device:TPU:2 now
where the time goes in v1:
time: 481 us
  blocking collectives  146 us (30%)
  local copies, waits for them, and re-layouts  132 us (27%)
  waiting for transfers between devices  70 us (15%)
  starting transfers between devices  49.3 us (10%)
  matrix products  47.9 us (10%)
  other arithmetic  21.6 us (4%)
  between operations  14.2 us (3%)
    unnamed x1, blocking collectives  91.5 us
    gather x4, local copies, waits for them, and re-layouts, one(): resp[:, blocks, :]  53.2 us
    gather x4, local copies, waits for them, and re-layouts, one(): adjo[:, blocks, :]  53.2 us
    ppermute x5, waiting for transfers between devices, collect(): theirs = lax.ppermute(grown, axis, [(d, d ^ reach) for d in range(ways)])  50.8 us
    ppermute x5, starting transfers between devices, collect(): theirs = lax.ppermute(grown, axis, [(d, d ^ reach) for d in range(ways)])  44.5 us
    psum x1, blocking collectives, body(): return lax.psum(mine, 'freq')  38.7 us
    dot_general x4, matrix products, one(): jnp.einsum('pksb,cpkb->cps', masked, adjo[:, blocks, :], preferred_elemen...  23.7 us
    dot_general x4, matrix products, one(): jnp.einsum('pksb,cpkb->cps', masked, resp[:, blocks, :], preferred_elemen...  23.7 us
  transfers between devices with their start and end apart: 7, of which 6 were waited for; matrix products, arithmetic and copies ran while one was open for 3% of the time, Pallas kernels for 0%

profile of v1, /device:TPU:2, one launch (start us, length us, event | category | flops | bytes accessed | tf_op | source)
XLA Modules:
  0.0 480.7 jit_solution(5774554216520176298)
XLA Ops:
  6.5 15.5 %all_to_all.36 = bf16[64,2,128]{2,1,0:T(2,128)(2,1)S(1)} all-to-all(bf16[64,2,128]{2,1,0:T(2,128)(2,1)} %param.9), channel_id=1, replica_groups=mesh['freq'=16,'patch'=32] {'freq'}, dimensions={0} | all-to-all | bytes 65536 | tf_op jit(solution)/shard_map/all_to_all | solution.py:58
  27.4 4.8 all-to-all-start.1
  32.2 6.2 %all-to-all-done.1 = bf16[64,2,128]{2,1,0:T(2,128)(2,1)S(1)} async-done(((bf16[64,2,128]{2,1,0:T(2,128)(2,1)}), bf16[64,2,128]{2,1,0:T(2,128)(2,1)S(1)}, u32[]{:S(2)}, u32[]{:S(2)}) %all-to-all-start.1) | async-done | bytes 32800 | tf_op jit(solution)/shard_map/all_to_all | solution.py:59
  39.4 5.2 %collective-permute-start.2 = (bf16[16,2,2048]{2,1,0:T(2,128)(2,1)S(1)}, bf16[16,2,2048]{2,1,0:T(2,128)(2,1)S(1)}, u32[]{:S(2)}, u32[]{:S(2)}) collective-permute-start(bf16[16,2,2048]{2,1,0:T(2,128)(2,1)S(1)} %broadcast_select_fusion.4), channel_id=1, source_target_pairs={{0,4},{1,5},{2,6},{3,7},{4,0},{5,1},{6,2},{7,3},{8,12},{9,13},{10,... | collective-permute-start | bytes 393224 | tf_op jit(solution)/shard_map/ppermute | solution.py:12
  45.3 4.4 collective-permute-done.2
  50.4 8.9 %collective-permute-start.3 = (bf16[32,2,2048]{2,1,0:T(2,128)(2,1)S(1)}, bf16[32,2,2048]{2,1,0:T(2,128)(2,1)S(1)}, u32[]{:S(2)}, u32[]{:S(2)}) collective-permute-start(bf16[32,2,2048]{2,1,0:T(2,128)(2,1)S(1)} %broadcast_select_fusion.3), channel_id=1, source_target_pairs={{0,8},{1,9},{2,10},{3,11},{4,12},{5,13},{6,14},{7,15},{8,0},{9,1},... | collective-permute-start | bytes 786440 | tf_op jit(solution)/shard_map/ppermute | solution.py:12
  62.9 16.6 %collective-permute-done.3 = bf16[32,2,2048]{2,1,0:T(2,128)(2,1)S(1)} collective-permute-done((bf16[32,2,2048]{2,1,0:T(2,128)(2,1)S(1)}, bf16[32,2,2048]{2,1,0:T(2,128)(2,1)S(1)}, u32[]{:S(2)}, u32[]{:S(2)}) %collective-permute-start.3) | collective-permute-done | bytes 262176 | tf_op jit(solution)/shard_map/ppermute | solution.py:12
  80.7 26.4 %collective-permute-start.4 = (bf16[64,2,2048]{2,1,0:T(2,128)(2,1)S(1)}, bf16[64,2,2048]{2,1,0:T(2,128)(2,1)S(1)}, u32[]{:S(2)}, u32[]{:S(2)}) collective-permute-start(bf16[64,2,2048]{2,1,0:T(2,128)(2,1)S(1)} %broadcast_select_fusion.2), channel_id=1, source_target_pairs={{0,16},{1,17},{2,18},{3,19},{4,20},{5,21},{6,22},{7,23},{8,24},{9,... | collective-permute-start | bytes 1572872 | tf_op jit(solution)/shard_map/ppermute | solution.py:12
  107.1 6.2 %broadcast_multiply_fusion = bf16[96,4,48,128]{3,2,1,0:T(8,128)(2,1)} fusion(bf16[96,4,48,128]{3,2,1,0:T(8,128)(2,1)} %param.11, bf16[96,4,48]{2,1,0:T(4,128)(2,1)S(1)} %and_convert_fusion), kind=kLoop, calls=%fused_computation.14 | loop fusion | flops 2359296 | bytes 9474048 | tf_op jit(solution)/shard_map/mul | solution.py:54
  113.3 28.6 %collective-permute-done.4 = bf16[64,2,2048]{2,1,0:T(2,128)(2,1)S(1)} collective-permute-done((bf16[64,2,2048]{2,1,0:T(2,128)(2,1)S(1)}, bf16[64,2,2048]{2,1,0:T(2,128)(2,1)S(1)}, u32[]{:S(2)}, u32[]{:S(2)}) %collective-permute-start.4) | collective-permute-done | bytes 524320 | tf_op jit(solution)/shard_map/ppermute | solution.py:12
  141.9 3.1 broadcast_select_fusion.1
  145.1 12.9 %all-gather.2.cloned.1.call-done = bf16[128,2,2048]{2,1,0:T(2,128)(2,1)} async-done(((bf16[4,2,2048]{2,1,0:T(2,128)(2,1)}), bf16[128,2,2048]{2,1,0:T(2,128)(2,1)}) %all-gather.2.cloned.1.call-update) | async-done | bytes 1048592 | tf_op jit(solution)/shard_map/all_gather | solution.py:66
  158.0 185.0 %while.14 = (s32[]{:T(128)}, f32[96]{0:T(128)S(1)}, bf16[128,2,2048]{2,1,0:T(2,128)(2,1)}, s32[96,4]{1,0:T(8,128)S(1)}, bf16[96,4,48,128]{3,2,1,0:T(8,128)(2,1)}...) while((s32[]{:T(128)}, f32[96]{0:T(128)S(1)}, ...), condition=%wide.region_2.3_spmd.clone, body=%wide.region_0.2_spmd.clone.sunk | while | flops 604571840 | bytes 59785376 | solution.py:46
  159.8 13.3 %gather_fusion = bf16[384,64,128]{2,1,0:T(8,128)(2,1)} fusion(bf16[64,16,128]{2,0,1:T(8,128)(2,1)S(1)} %copy.39, s32[1024]{0:T(1024)S(1)} %pad_clamp_fusion.2), kind=kCustom, calls=%fused_computation.1.clone.clone.1 | custom fusion | bytes 12584448 | tf_op jit(solution)/shard_map/while/body/eval_jaxpr/gather | solution.py:39
  173.1 5.9 %convolution_bitcast_fusion.4 = f32[64,96,48]{0,2,1:T(8,128)S(1)} fusion(bf16[64,96,4,128]{3,0,2,1:T(8,128)(2,1)} %bitcast.66, bf16[96,4,48,128]{3,2,1,0:T(8,128)(2,1)} %get-tuple-element.233), kind=kOutput, calls=%fused_computation.2.clone.1 | convolution fusion | flops 301989888 | bytes 12189696 | tf_op jit(solution)/shard_map/while/body/eval_jaxpr/pksb,cpkb->cps/dot_general | solution.py:38
  181.1 13.3 %gather_fusion.1 = bf16[384,64,128]{2,1,0:T(8,128)(2,1)} fusion(bf16[64,16,128]{2,0,1:T(8,128)(2,1)S(1)} %copy.41, s32[1024]{0:T(1024)S(1)} %pad_clamp_fusion.2), kind=kCustom, calls=%fused_computation.clone.clone.1 | custom fusion | bytes 12584448 | tf_op jit(solution)/shard_map/while/body/eval_jaxpr/gather | solution.py:36
  194.4 5.9 %convolution_bitcast_fusion.5 = f32[64,96,48]{0,2,1:T(8,128)S(1)} fusion(bf16[64,96,4,128]{3,0,2,1:T(8,128)(2,1)} %bitcast.65, bf16[96,4,48,128]{3,2,1,0:T(8,128)(2,1)} %get-tuple-element.233), kind=kOutput, calls=%fused_computation.3.clone.1 | convolution fusion | flops 301989888 | bytes 12189696 | tf_op jit(solution)/shard_map/while/body/eval_jaxpr/pksb,cpkb->cps/dot_general | solution.py:35
  202.2 2.1 fusion.23
  206.1 13.3 %gather_fusion = bf16[384,64,128]{2,1,0:T(8,128)(2,1)} fusion(bf16[64,16,128]{2,0,1:T(8,128)(2,1)S(1)} %copy.39, s32[1024]{0:T(1024)S(1)} %pad_clamp_fusion.2), kind=kCustom, calls=%fused_computation.1.clone.clone.1 | custom fusion | bytes 12584448 | tf_op jit(solution)/shard_map/while/body/eval_jaxpr/gather | solution.py:39
  219.4 5.9 %convolution_bitcast_fusion.4 = f32[64,96,48]{0,2,1:T(8,128)S(1)} fusion(bf16[64,96,4,128]{3,0,2,1:T(8,128)(2,1)} %bitcast.66, bf16[96,4,48,128]{3,2,1,0:T(8,128)(2,1)} %get-tuple-element.233), kind=kOutput, calls=%fused_computation.2.clone.1 | convolution fusion | flops 301989888 | bytes 12189696 | tf_op jit(solution)/shard_map/while/body/eval_jaxpr/pksb,cpkb->cps/dot_general | solution.py:38
  227.4 13.3 %gather_fusion.1 = bf16[384,64,128]{2,1,0:T(8,128)(2,1)} fusion(bf16[64,16,128]{2,0,1:T(8,128)(2,1)S(1)} %copy.41, s32[1024]{0:T(1024)S(1)} %pad_clamp_fusion.2), kind=kCustom, calls=%fused_computation.clone.clone.1 | custom fusion | bytes 12584448 | tf_op jit(solution)/shard_map/while/body/eval_jaxpr/gather | solution.py:36
  240.7 5.9 %convolution_bitcast_fusion.5 = f32[64,96,48]{0,2,1:T(8,128)S(1)} fusion(bf16[64,96,4,128]{3,0,2,1:T(8,128)(2,1)} %bitcast.65, bf16[96,4,48,128]{3,2,1,0:T(8,128)(2,1)} %get-tuple-element.233), kind=kOutput, calls=%fused_computation.3.clone.1 | convolution fusion | flops 301989888 | bytes 12189696 | tf_op jit(solution)/shard_map/while/body/eval_jaxpr/pksb,cpkb->cps/dot_general | solution.py:35
  252.3 13.3 %gather_fusion = bf16[384,64,128]{2,1,0:T(8,128)(2,1)} fusion(bf16[64,16,128]{2,0,1:T(8,128)(2,1)S(1)} %copy.39, s32[1024]{0:T(1024)S(1)} %pad_clamp_fusion.2), kind=kCustom, calls=%fused_computation.1.clone.clone.1 | custom fusion | bytes 12584448 | tf_op jit(solution)/shard_map/while/body/eval_jaxpr/gather | solution.py:39
  265.6 5.9 %convolution_bitcast_fusion.4 = f32[64,96,48]{0,2,1:T(8,128)S(1)} fusion(bf16[64,96,4,128]{3,0,2,1:T(8,128)(2,1)} %bitcast.66, bf16[96,4,48,128]{3,2,1,0:T(8,128)(2,1)} %get-tuple-element.233), kind=kOutput, calls=%fused_computation.2.clone.1 | convolution fusion | flops 301989888 | bytes 12189696 | tf_op jit(solution)/shard_map/while/body/eval_jaxpr/pksb,cpkb->cps/dot_general | solution.py:38
  273.6 13.3 %gather_fusion.1 = bf16[384,64,128]{2,1,0:T(8,128)(2,1)} fusion(bf16[64,16,128]{2,0,1:T(8,128)(2,1)S(1)} %copy.41, s32[1024]{0:T(1024)S(1)} %pad_clamp_fusion.2), kind=kCustom, calls=%fused_computation.clone.clone.1 | custom fusion | bytes 12584448 | tf_op jit(solution)/shard_map/while/body/eval_jaxpr/gather | solution.py:36
  286.9 5.9 %convolution_bitcast_fusion.5 = f32[64,96,48]{0,2,1:T(8,128)S(1)} fusion(bf16[64,96,4,128]{3,0,2,1:T(8,128)(2,1)} %bitcast.65, bf16[96,4,48,128]{3,2,1,0:T(8,128)(2,1)} %get-tuple-element.233), kind=kOutput, calls=%fused_computation.3.clone.1 | convolution fusion | flops 301989888 | bytes 12189696 | tf_op jit(solution)/shard_map/while/body/eval_jaxpr/pksb,cpkb->cps/dot_general | solution.py:35
  298.6 13.3 %gather_fusion = bf16[384,64,128]{2,1,0:T(8,128)(2,1)} fusion(bf16[64,16,128]{2,0,1:T(8,128)(2,1)S(1)} %copy.39, s32[1024]{0:T(1024)S(1)} %pad_clamp_fusion.2), kind=kCustom, calls=%fused_computation.1.clone.clone.1 | custom fusion | bytes 12584448 | tf_op jit(solution)/shard_map/while/body/eval_jaxpr/gather | solution.py:39
  311.9 5.9 %convolution_bitcast_fusion.4 = f32[64,96,48]{0,2,1:T(8,128)S(1)} fusion(bf16[64,96,4,128]{3,0,2,1:T(8,128)(2,1)} %bitcast.66, bf16[96,4,48,128]{3,2,1,0:T(8,128)(2,1)} %get-tuple-element.233), kind=kOutput, calls=%fused_computation.2.clone.1 | convolution fusion | flops 301989888 | bytes 12189696 | tf_op jit(solution)/shard_map/while/body/eval_jaxpr/pksb,cpkb->cps/dot_general | solution.py:38
  319.9 13.3 %gather_fusion.1 = bf16[384,64,128]{2,1,0:T(8,128)(2,1)} fusion(bf16[64,16,128]{2,0,1:T(8,128)(2,1)S(1)} %copy.41, s32[1024]{0:T(1024)S(1)} %pad_clamp_fusion.2), kind=kCustom, calls=%fused_computation.clone.clone.1 | custom fusion | bytes 12584448 | tf_op jit(solution)/shard_map/while/body/eval_jaxpr/gather | solution.py:36
  333.2 5.9 %convolution_bitcast_fusion.5 = f32[64,96,48]{0,2,1:T(8,128)S(1)} fusion(bf16[64,96,4,128]{3,0,2,1:T(8,128)(2,1)} %bitcast.65, bf16[96,4,48,128]{3,2,1,0:T(8,128)(2,1)} %get-tuple-element.233), kind=kOutput, calls=%fused_computation.3.clone.1 | convolution fusion | flops 301989888 | bytes 12189696 | tf_op jit(solution)/shard_map/while/body/eval_jaxpr/pksb,cpkb->cps/dot_general | solution.py:35
  343.6 91.5 %all-reduce = f32[3072]{0:T(1024)S(1)} all-reduce(f32[3072]{0:T(1024)S(1)} %bitcast.73), channel_id=2, replica_groups=mesh['freq'=16,'patch'=32] {'patch'}, use_global_device_ids=true, to_apply=%region_3.4.clone | all-reduce | flops 3072 | bytes 24576
  435.2 38.7 %psum.7 = f32[96]{0:T(128)} all-reduce(f32[96]{0:T(128)S(1)} %dynamic-slice.1), channel_id=1, replica_groups=mesh['freq'=16,'patch'=32] {'freq'}, use_global_device_ids=true, to_apply=%region_4.5 | all-reduce | flops 96 | bytes 768 | tf_op jit(solution)/shard_map/psum | solution.py:75
  (71 shorter events, 41.3 us)
Async XLA Ops:
  22.0 3.1 collective-permute-start
  25.3 13.8 %collective-permute-start.1 = (bf16[8,2,2048]{2,1,0:T(2,128)(2,1)S(1)}, bf16[8,2,2048]{2,1,0:T(2,128)(2,1)S(1)}, u32[]{:S(2)}, u32[]{:S(2)}) collective-permute-start(bf16[8,2,2048]{2,1,0:T(2,128)(2,1)S(1)} %broadcast_select_fusion.5), channel_id=1, source_target_pairs={{0,2},{1,3},{2,0},{3,1},{4,6},{5,7},{6,4},{7,5},{8,10},{9,11},{10,... | collective-permute-start | bytes 196616 | tf_op jit(solution)/shard_map/ppermute | solution.py:12
  27.4 11.1 %all-to-all-start.1 = ((bf16[64,2,128]{2,1,0:T(2,128)(2,1)}), bf16[64,2,128]{2,1,0:T(2,128)(2,1)S(1)}, u32[]{:S(2)}, u32[]{:S(2)}) async-start(bf16[64,2,128]{2,1,0:T(2,128)(2,1)} %param.10), calls=%async_computation.1 | async-start | bytes 65536 | tf_op jit(solution)/shard_map/all_to_all | solution.py:59
  32.1 125.9 %all-gather.2.cloned.1.call-start = ((), (), s32[]{:S(2)}) async-start(), calls=%async_computation.2 | async-start | bytes 1081344 | tf_op jit(solution)/shard_map/all_gather | solution.py:66
  39.4 10.4 %collective-permute-start.2 = (bf16[16,2,2048]{2,1,0:T(2,128)(2,1)S(1)}, bf16[16,2,2048]{2,1,0:T(2,128)(2,1)S(1)}, u32[]{:S(2)}, u32[]{:S(2)}) collective-permute-start(bf16[16,2,2048]{2,1,0:T(2,128)(2,1)S(1)} %broadcast_select_fusion.4), channel_id=1, source_target_pairs={{0,4},{1,5},{2,6},{3,7},{4,0},{5,1},{6,2},{7,3},{8,12},{9,13},{10,... | collective-permute-start | bytes 393224 | tf_op jit(solution)/shard_map/ppermute | solution.py:12
  50.4 29.1 %collective-permute-start.3 = (bf16[32,2,2048]{2,1,0:T(2,128)(2,1)S(1)}, bf16[32,2,2048]{2,1,0:T(2,128)(2,1)S(1)}, u32[]{:S(2)}, u32[]{:S(2)}) collective-permute-start(bf16[32,2,2048]{2,1,0:T(2,128)(2,1)S(1)} %broadcast_select_fusion.3), channel_id=1, source_target_pairs={{0,8},{1,9},{2,10},{3,11},{4,12},{5,13},{6,14},{7,15},{8,0},{9,1},... | collective-permute-start | bytes 786440 | tf_op jit(solution)/shard_map/ppermute | solution.py:12
  80.7 61.3 %collective-permute-start.4 = (bf16[64,2,2048]{2,1,0:T(2,128)(2,1)S(1)}, bf16[64,2,2048]{2,1,0:T(2,128)(2,1)S(1)}, u32[]{:S(2)}, u32[]{:S(2)}) collective-permute-start(bf16[64,2,2048]{2,1,0:T(2,128)(2,1)S(1)} %broadcast_select_fusion.2), channel_id=1, source_target_pairs={{0,16},{1,17},{2,18},{3,19},{4,20},{5,21},{6,22},{7,23},{8,24},{9,... | collective-permute-start | bytes 1572872 | tf_op jit(solution)/shard_map/ppermute | solution.py:12
  158.0 185.1 %copy-start = (s32[96]{0:T(128)S(1)}, s32[96]{0:T(128)}, u32[]{:S(2)}) copy-start(s32[96]{0:T(128)} %param.15) | copy-start | bytes 1156
Sparse Core Ops, SparseCore 0:
  39.2 118.7 all-gather.1
